TPU v7x, 32 devices: a whole 2x2x4 slice. The times are simulated.
32 devices in a mesh: row: 8 (over y, x, core), col: 4 (over z).
Axes of the slice: x: 2, y: 2, z: 4, core: 2. Of those that a mesh axis runs over, the one named last changes fastest.
Arguments:
- amplitudes: bfloat16 [64, 6400], P(('col', 'row')), may hold values from -6 to 6
- panel: bfloat16 [9600, 6400], P('col', 'row'), may hold values from -0.21875 to 0.21875
- irrep_ij: int32 [64], replicated, may hold values from 0 to 7
- irrep_ef: int32 [6400], replicated, may hold values from 0 to 7
Outputs:
- ladder: bfloat16 [64, 9600], P(('col', 'row'))
All inputs are finite; a program needn't handle non-finite values.
Results may differ from a plain program's by a relative error of at most 0.003.
Values may be sent and summed in bfloat16 or wider, within the bound.
A program may use at most 64 MiB of HBM per device.

v0:
```python
import jax
import jax.numpy as jnp
from jax import lax
from jax.sharding import PartitionSpec as P


def contract(left, right):
    return lax.dot_general(
        left, right, (((1,), (1,)), ((), ())), preferred_element_type=jnp.float32
    )


def ef_local(irrep_ij, irrep_ef, blocked):
    pair_rows = blocked.shape[0]
    pair_cols = blocked.shape[1]
    col_index = lax.axis_index("col")
    row_index = lax.axis_index("row")
    sym_rows = lax.dynamic_slice_in_dim(irrep_ij, col_index * pair_rows, pair_rows)
    sym_cols = lax.dynamic_slice_in_dim(irrep_ef, row_index * pair_cols, pair_cols)
    return jnp.where(sym_rows[:, None] == sym_cols[None, :], blocked, jnp.zeros_like(blocked))


def body(amplitudes, panel, irrep_ij, irrep_ef):
    blocked = lax.all_to_all(amplitudes, "row", split_axis=1, concat_axis=0, tiled=True)
    allowed = ef_local(irrep_ij, irrep_ef, blocked)
    partial_terms = contract(allowed, lax.all_gather(panel, "col", axis=0, tiled=True))
    summed = lax.psum_scatter(partial_terms, "row", scatter_dimension=0, tiled=True)
    return summed.astype(jnp.bfloat16)


def solution(mesh):
    in_specs = (P(("col", "row"), None), P("col", "row"), P(), P())
    out_specs = P(("col", "row"), None)
    return jax.shard_map(body, mesh=mesh, in_specs=in_specs, out_specs=out_specs, check_vma=False)
```

profile of v0, /device:TPU:0, one launch (start us, length us, event | category | flops | bytes accessed | tf_op | source)
XLA Modules:
  0.0 396.6 jit_solution(6917603864206018929)
XLA Ops:
  6.5 0.0 all-gather.3.cloned.1.call-start
  6.5 0.7 all-gather.3.cloned.1.call-update
  7.3 0.8 all_to_all.14
  8.1 0.6 copy.7
  8.7 5.2 %all-to-all-start = ((bf16[2,8,800]{2,0,1:T(2,128)(2,1)}), bf16[2,8,800]{2,0,1:T(2,128)(2,1)S(1)}, u32[]{:S(2)}, u32[]{:S(2)}) async-start(bf16[2,8,800]{2,0,1:T(2,128)(2,1)} %copy.7), calls=%async_computation | async-start | bytes 57344 | tf_op jit(solution)/shard_map/all_to_all | solution.py:24
  13.9 0.8 dynamic_slice.7
  14.7 0.7 dynamic_slice.6
  15.4 1.2 dynamic-slice
  17.2 1.5 all-to-all-done
  18.8 259.8 %all-gather.3.cloned.1.call-done = bf16[4,2400,800]{1,2,0:T(8,128)(2,1)} async-done(((bf16[1,2400,800]{1,2,0:T(8,128)(2,1)}), bf16[4,2400,800]{1,2,0:T(8,128)(2,1)}) %all-gather.3.cloned.1.call-update) | async-done | bytes 15360016 | tf_op jit(solution)/shard_map/all_gather | solution.py:26
  278.6 48.0 %copy.8 = bf16[4,2400,800]{1,0,2:T(4,128)(2,1)} copy(bf16[4,2400,800]{1,2,0:T(8,128)(2,1)} %all-gather.3.cloned.1.call-done) | data formatting | bytes 30720000 | tf_op jit(solution)/shard_map/all_gather | solution.py:26
  326.6 24.8 %reshape.6 = bf16[9600,800]{0,1:T(8,128)(2,1)} reshape(bf16[4,2400,800]{1,0,2:T(4,128)(2,1)} %copy.8) | data formatting | bytes 30720000
  351.5 6.6 %fusion = f32[16,9600]{1,0:T(8,128)S(1)} fusion(bf16[9600,800]{0,1:T(8,128)(2,1)} %reshape.6, bf16[16,800]{1,0:T(8,128)(2,1)S(1)} %all_to_all.17, s32[800]{0:T(1024)S(1)} %dynamic_slice.7, s32[16]{0:T(128)S(1)} %dynamic_slice.6), kind=kOutput, calls=%fused_computation.2 | convolution fusion | flops 245785600 | bytes 16003264 | tf_op jit(solution)/shard_map/dot_general | solution.py:8
  358.1 31.0 %all-reduce.2 = bf16[16,9600]{1,0:T(8,128)(2,1)S(1)} all-reduce(f32[16,9600]{1,0:T(8,128)S(1)} %fusion), channel_id=2, replica_groups=mesh['row'=8,'col'=4] {'row'}, use_global_device_ids=true, to_apply=%region_0.1.clone | all-reduce | flops 153600 | bytes 921600
  389.1 0.7 dynamic-slice_convert_fusion
  (1 shorter events, 0.0 us)
Async XLA Ops:
  6.5 272.1 %all-gather.3.cloned.1.call-start = ((), (), s32[]{:S(2)}) async-start(), calls=%async_computation.1 | async-start | bytes 19456000 | tf_op jit(solution)/shard_map/all_gather | solution.py:26
  8.7 10.0 %all-to-all-start = ((bf16[2,8,800]{2,0,1:T(2,128)(2,1)}), bf16[2,8,800]{2,0,1:T(2,128)(2,1)S(1)}, u32[]{:S(2)}, u32[]{:S(2)}) async-start(bf16[2,8,800]{2,0,1:T(2,128)(2,1)} %copy.7), calls=%async_computation | async-start | bytes 57344 | tf_op jit(solution)/shard_map/all_to_all | solution.py:24
Sparse Core Ops, SparseCore 0:
  8.9 269.6 all-gather.2
where the time goes:
time: 398 us; the launch traced here: 397 us
  waiting for transfers between devices  262 us (66%)
  local copies, waits for them, and re-layouts  77.8 us (20%)
  blocking collectives  31 us (8%)
  between operations  14 us (4%)
  matrix products  6.61 us (2%)
  starting transfers between devices  5.17 us (1%)
    all_gather x1, waiting for transfers between devices, body(): lax.all_gather(panel, 'col', axis=0, tiled=True)  260 us
    all_gather x1, local copies, waits for them, and re-layouts, body(): lax.all_gather(panel, 'col', axis=0, tiled=True)  48 us
    unnamed x1, blocking collectives  31 us
    unnamed x2, local copies, waits for them, and re-layouts  26.1 us
  transfers between devices with their start and end apart: 2, of which 2 were waited for; matrix products, arithmetic and copies ran while one was open for 1% of the time, Pallas kernels for 0%

commit v1 on v0

v1 whole, which is shorter than its diff:
```python
import functools

import jax
import jax.numpy as jnp
from jax import lax
from jax.experimental import pallas as pl
from jax.experimental.pallas import tpu as pltpu
from jax.sharding import PartitionSpec as P

TILE = 512


def tiles(ab):
    return [(at, min(TILE, ab - at)) for at in range(0, ab, TILE)]


def remote(src, dst, send_sem, recv_sem, **device):
    return pltpu.make_async_remote_copy(
        src_ref=src, dst_ref=dst, send_sem=send_sem, recv_sem=recv_sem,
        device_id=device, device_id_type=pl.DeviceIdType.MESH,
    )


def kernel(R, C, amp_ref, sym_ij_ref, sym_ef_ref, panel_ref, out_ref,
           panel_v, slabs, met, rows16, gathered, allowed, part, from_pair, summed, from_chips, outgoing, landed,
           panel_sem, s1, r1, s2, r2, s3, r3, s4, r4, s5, r5):
    r = lax.axis_index("row")
    c = lax.axis_index("col")
    k = lax.rem(r, 2)
    q = r // 2
    Q = R // 2
    J, EF = amp_ref.shape
    ef = EF // R
    ab = panel_v.shape[1]

    load = pltpu.make_async_copy(panel_ref, panel_v, panel_sem)
    load.start()

    barrier = pltpu.get_barrier_semaphore()
    for d in range(1, R):
        pl.semaphore_signal(barrier, inc=1, device_id={"row": lax.rem(r + d, R)}, device_id_type=pl.DeviceIdType.MESH)
    for d in range(1, C):
        pl.semaphore_signal(barrier, inc=1, device_id={"col": lax.rem(c + d, C)}, device_id_type=pl.DeviceIdType.MESH)

    first = (c * R + r) * J
    sym_ef = sym_ef_ref[...].reshape(1, EF)
    which = lax.broadcasted_iota(jnp.int32, (J, EF), 0)
    sym_ij = jnp.full((J, EF), sym_ij_ref[first], jnp.int32)
    for j in range(1, J):
        sym_ij = jnp.where(which == j, sym_ij_ref[first + j], sym_ij)
    masked = jnp.where(sym_ij == sym_ef, amp_ref[...].astype(jnp.float32), 0.0)
    for p in range(R):
        slabs[p] = masked[:, p * ef:(p + 1) * ef]

    pl.semaphore_wait(barrier, R + C - 2)

    sends = []
    for d in range(1, R):
        to = lax.rem(r + d, R)
        send = remote(slabs.at[to], met.at[r], s1.at[d], r1.at[d], row=to)
        send.start()
        sends.append(send)
    met[r] = slabs[r]
    for send in sends:
        send.wait_recv()
    for p in range(R):
        rows16[pl.ds(p * J, J), :] = met[p]
    gathered[c] = rows16[...].astype(jnp.bfloat16)

    more = []
    for d in range(1, C):
        to = lax.rem(c + d, C)
        send = remote(gathered.at[c], gathered.at[c], s2.at[d], r2.at[d], col=to)
        send.start()
        more.append(send)

    total_rows = R * C * J
    group = next(g for g in (8, 4, 2, 1) if Q % min(g, Q) == 0 and min(g, Q) * C * J <= 256)
    group = min(group, Q)
    picks = []
    for half in range(2):
        for start in range(0, Q, group):
            blocks = []
            for p in range(start, start + group):
                at = lax.broadcasted_iota(jnp.int32, (C * J, total_rows), 0)
                source = (at // J) * (R * J) + (2 * p + half) * J + lax.rem(at, J)
                blocks.append(source == lax.broadcasted_iota(jnp.int32, (C * J, total_rows), 1))
            picks.append((half, start, blocks))

    for send in more:
        send.wait_recv()
    everything = gathered[...].reshape(total_rows, ef)
    for half, start, blocks in picks:
        pick = jnp.concatenate([jnp.where(b, 1.0, 0.0) for b in blocks], axis=0).astype(jnp.bfloat16)
        allowed[half, pl.ds(start * C * J, group * C * J), :] = jnp.dot(
            pick, everything, preferred_element_type=jnp.float32
        ).astype(jnp.bfloat16)

    def multiply(half):
        left = allowed[half]
        for at, size in tiles(ab):
            part[half, :, pl.ds(at, size)] = lax.dot_general(
                left, panel_v[:, pl.ds(at, size)], (((1,), (0,)), ((), ())), preferred_element_type=jnp.float32
            )

    load.wait()
    multiply(1 - k)
    pair = remote(part.at[1 - k], from_pair, s3, r3, row=2 * q + 1 - k)
    pair.start()
    multiply(k)
    pair.wait_recv()

    for p in range(Q):
        at = pl.ds(p * C * J, C * J)
        summed[p] = part[k, at, :] + from_pair[at, :]
    chips = []
    for d in range(1, Q):
        to = lax.rem(q + d, Q)
        send = remote(summed.at[to], from_chips.at[d - 1], s4.at[d], r4.at[d], row=2 * to + k)
        send.start()
        chips.append(send)
    total = summed[q]
    for d, send in enumerate(chips):
        send.wait_recv()
        total = total + from_chips[d]
    for p in range(C):
        outgoing[p] = total[p * J:(p + 1) * J, :]
    last = []
    for d in range(1, C):
        to = lax.rem(c + d, C)
        send = remote(outgoing.at[to], landed.at[c], s5.at[d], r5.at[d], col=to)
        send.start()
        last.append(send)
    landed[c] = outgoing[c]
    for send in last:
        send.wait_recv()
    for p in range(C):
        out_ref[:, p * ab:(p + 1) * ab] = landed[p].astype(jnp.bfloat16)
    pair.wait_send()
    for send in sends + more + chips + last:
        send.wait_send()


def solution(mesh):
    R, C = mesh.shape["row"], mesh.shape["col"]

    def body(amplitudes, panel, irrep_ij, irrep_ef):
        J, EF = amplitudes.shape
        ab, ef = panel.shape
        Q = R // 2
        H = Q * C * J
        f32, bf16 = jnp.float32, jnp.bfloat16
        dma = pltpu.SemaphoreType.DMA
        return pl.pallas_call(
            functools.partial(kernel, R, C),
            out_shape=jax.ShapeDtypeStruct((J, C * ab), bf16),
            in_specs=[
                pl.BlockSpec(memory_space=pltpu.VMEM),
                pl.BlockSpec(memory_space=pltpu.SMEM),
                pl.BlockSpec(memory_space=pltpu.VMEM),
                pl.BlockSpec(memory_space=pl.ANY),
            ],
            out_specs=pl.BlockSpec(memory_space=pltpu.VMEM),
            scratch_shapes=[
                pltpu.VMEM((ef, ab), bf16),
                pltpu.VMEM((R, J, ef), f32),
                pltpu.VMEM((R, J, ef), f32),
                pltpu.VMEM((R * J, ef), f32),
                pltpu.VMEM((C, R * J, ef), bf16),
                pltpu.VMEM((2, H, ef), bf16),
                pltpu.VMEM((2, H, ab), f32),
                pltpu.VMEM((H, ab), f32),
                pltpu.VMEM((Q, C * J, ab), f32),
                pltpu.VMEM((max(Q - 1, 1), C * J, ab), f32),
                pltpu.VMEM((C, J, ab), f32),
                pltpu.VMEM((C, J, ab), f32),
                dma,
                dma((R,)), dma((R,)),
                dma((C,)), dma((C,)),
                dma, dma,
                dma((Q,)), dma((Q,)),
                dma((C,)), dma((C,)),
            ],
            compiler_params=pltpu.CompilerParams(
                collective_id=0, has_side_effects=True, vmem_limit_bytes=60 << 20
            ),
            cost_estimate=pl.CostEstimate(
                flops=2 * R * C * J * ef * ab, bytes_accessed=2 * ab * ef, transcendentals=0
            ),
        )(amplitudes, irrep_ij, irrep_ef, panel.T)

    in_specs = (P(("col", "row"), None), P("col", "row"), P(), P())
    return jax.shard_map(body, mesh=mesh, in_specs=in_specs, out_specs=P(("col", "row"), None), check_vma=False)
```

time: 398 us -> 28.6 us (0.07)
  waiting for transfers between devices: 262 us -> 0 us
  local copies, waits for them, and re-layouts: 77.8 us -> 1.42 us
  blocking collectives: 31 us -> 0 us
  Pallas kernels: 0 us -> 26.9 us
  between operations: 14 us -> 0.01 us
  matrix products: 6.61 us -> 0 us
  starting transfers between devices: 5.17 us -> 0 us
    all_gather x1 -> x0, waiting for transfers between devices: 260 us -> none  [body(): lax.all_gather(panel, 'col', axis=0, tiled=True)]
    all_gather x1 -> x0, local copies, waits for them, and re-layouts: 48 us -> none  [body(): lax.all_gather(panel, 'col', axis=0, tiled=True)]
    unnamed x1 -> x0, blocking collectives: 31 us -> none
    pallas_call x0 -> x1, Pallas kernels: none -> 26.9 us  [body(): pl.pallas_call(functools.partial(kernel, R, C), out_shape=jax.ShapeDtypeS...]
    unnamed x2 -> x1, local copies, waits for them, and re-layouts: 26.1 us -> 1.42 us
    dot_general x1 -> x0, matrix products: 6.61 us -> none  [contract(): lax.dot_general(left, right, (((1,), (1,)), ((), ())), preferred_element_...]
    all_to_all x1 -> x0, starting transfers between devices: 5.17 us -> none  [body(): lax.all_to_all(amplitudes, 'row', split_axis=1, concat_axis=0, tiled=True)]
  transfers between devices with their start and end apart: 2 -> 0, of which waited for: 2 -> 0; matrix products, arithmetic and copies ran while one was open for 1% -> 0% of each run, Pallas kernels for 0% -> 0%
where the time goes in v1:
time: 28.6 us; the launch traced here: 28.4 us
  Pallas kernels  26.9 us (94%)
  local copies, waits for them, and re-layouts  1.42 us (5%)
    pallas_call x1, Pallas kernels, body(): pl.pallas_call(functools.partial(kernel, R, C), out_shape=jax.ShapeDtypeS...  26.9 us
    unnamed x1, local copies, waits for them, and re-layouts  1.42 us

profile of v1, /device:TPU:0, one launch (start us, length us, event | category | flops | bytes accessed | tf_op | source)
XLA Modules:
  0.0 28.4 jit_solution(6784939278257119550)
XLA Ops:
  0.0 26.9 %shard_map.46 = bf16[2,9600]{1,0:T(2,128)(2,1)} custom-call(bf16[2,6400]{1,0:T(2,128)(2,1)} %amp_ref.1, s32[64]{0:T(128)} %sym_ij_ref.1, s32[6400]{0:T(1024)} %sym_ef_ref.1, bf16[800,2400]{1,0:T(8,128)(2,1)} %bitcast.1), custom_call_target="tpu_custom_call" | custom-call | flops 245760000 | bytes 3840000 | tf_op jit(solution)/shard_map/pallas_call | solution.py:154
  26.9 1.4 %copy.6 = bf16[2,9600]{1,0:T(2,128)(2,1)} copy(bf16[2,9600]{1,0:T(2,128)(2,1)} %shard_map.46) | data formatting | bytes 76800

commit v2 on v1

--- a/solution.py
+++ b/solution.py
@@ -7,11 +7,12 @@
 from jax.experimental.pallas import tpu as pltpu
 from jax.sharding import PartitionSpec as P
 
-TILE = 512
-
-
-def tiles(ab):
-    return [(at, min(TILE, ab - at)) for at in range(0, ab, TILE)]
+CHUNKS = 3
+
+
+def chunks(ab, n):
+    step = ab // n // 128 * 128
+    return [(j * step, step if j < n - 1 else ab - j * step) for j in range(n)]
 
 
 def remote(src, dst, send_sem, recv_sem, **device):
@@ -21,7 +22,129 @@
     )
 
 
-def kernel(R, C, amp_ref, sym_ij_ref, sym_ef_ref, panel_ref, out_ref,
+def direct(R, C, N, amp_ref, sym_ij_ref, sym_ef_ref, panel_ref, out_ref,
+           panel_v, wide, slabs, pick, gathered, allowed, part, from_pair, summed, from_chips, outgoing, landed,
+           panel_sem, s1, r1, s3, r3, s4, r4, s5, r5):
+    r = lax.axis_index("row")
+    c = lax.axis_index("col")
+    k = lax.rem(r, 2)
+    q = r // 2
+    Q = R // 2
+    J, EF = amp_ref.shape
+    ef = EF // R
+    ab = panel_v.shape[1]
+
+    load = pltpu.make_async_copy(panel_ref, panel_v, panel_sem)
+    load.start()
+
+    lanes = [(at, min(128, ef - at)) for at in range(0, ef, 128)]
+    L = 8
+    D = R * C
+    peers = [(dr, dc) for dc in reversed(range(C)) for dr in reversed(range(R)) if (dr, dc) != (0, 0)]
+
+    barrier = pltpu.get_barrier_semaphore()
+    for dr, dc in peers:
+        pl.semaphore_signal(
+            barrier, inc=1, device_id={"row": lax.rem(r + dr, R), "col": lax.rem(c + dc, C)},
+            device_id_type=pl.DeviceIdType.MESH,
+        )
+
+    first = (c * R + r) * J
+    sym_ef = sym_ef_ref[...].reshape(1, EF)
+    which = lax.broadcasted_iota(jnp.int32, (J, EF), 0)
+    sym_ij = jnp.full((J, EF), sym_ij_ref[first], jnp.int32)
+    for j in range(1, J):
+        sym_ij = jnp.where(which == j, sym_ij_ref[first + j], sym_ij)
+    masked = jnp.where(sym_ij == sym_ef, amp_ref[...].astype(jnp.float32), 0.0)
+    wide[...] = jnp.zeros_like(wide)
+    for p in range(R):
+        for i, (at, size) in enumerate(lanes):
+            for j in range(J):
+                wide[p, j * L + i:j * L + i + 1, 0:size] = masked[j:j + 1, p * ef + at:p * ef + at + size]
+    slabs[...] = wide[...].astype(jnp.bfloat16)
+
+    at = lax.broadcasted_iota(jnp.int32, (C * J, D * J * L), 0)
+    held = lax.broadcasted_iota(jnp.int32, (C * J, D * J * L), 1)
+    base = (at // J) * (R * J * L) + lax.rem(at, J) * L
+    for half in range(2):
+        for p in range(Q):
+            for i in range(len(lanes)):
+                pick[i, half, pl.ds(p * C * J, C * J), :] = jnp.where(
+                    base + ((2 * p + half) * J * L + i) == held, 1.0, 0.0)
+    picks = pick[...].reshape(len(lanes) * D * J, D * J * L).astype(jnp.bfloat16)
+
+    pl.semaphore_wait(barrier, D - 1)
+
+    sends = []
+    for dr, dc in peers:
+        row, col = lax.rem(r + dr, R), lax.rem(c + dc, C)
+        send = remote(slabs.at[row], gathered.at[c * R + r], s1.at[dc * R + dr], r1.at[dc * R + dr], row=row, col=col)
+        send.start()
+        sends.append(send)
+    gathered[c * R + r] = slabs[r]
+    for send in sends:
+        send.wait_recv()
+    picked = jnp.dot(picks, gathered[...].reshape(D * J * L, 128), preferred_element_type=jnp.float32)
+    for i, (at, size) in enumerate(lanes):
+        for half in range(2):
+            start = (i * 2 + half) * Q * C * J
+            allowed[half, :, at:at + size] = picked[start:start + Q * C * J, :size].astype(jnp.bfloat16)
+
+    cuts = chunks(ab, N)
+
+    def multiply(half, j):
+        at, size = cuts[j]
+        part[j][half] = jnp.dot(allowed[half], panel_v[:, pl.ds(at, size)], preferred_element_type=jnp.float32)
+
+    load.wait()
+    pairs, chips, last = [], [], []
+
+    def reduce_pair(j):
+        pairs[j].wait_recv()
+        for p in range(Q):
+            at = pl.ds(p * C * J, C * J)
+            summed[j][p] = part[j][k, at, :] + from_pair[j][at, :]
+        chips.append([])
+        for d in range(1, Q):
+            to = lax.rem(q + d, Q)
+            send = remote(summed[j].at[to], from_chips[j].at[d - 1], s4.at[j, d], r4.at[j, d], row=2 * to + k)
+            send.start()
+            chips[j].append(send)
+
+    for j in range(len(cuts)):
+        multiply(1 - k, j)
+        pair = remote(part[j].at[1 - k], from_pair[j], s3.at[j], r3.at[j], row=2 * q + 1 - k)
+        pair.start()
+        pairs.append(pair)
+        multiply(k, j)
+        if j > 0:
+            reduce_pair(j - 1)
+    reduce_pair(len(cuts) - 1)
+
+    for j in range(len(cuts)):
+        total = summed[j][q]
+        for d, send in enumerate(chips[j]):
+            send.wait_recv()
+            total = total + from_chips[j][d]
+        for p in range(C):
+            outgoing[j][p] = total[p * J:(p + 1) * J, :]
+        last.append([])
+        for d in range(1, C):
+            to = lax.rem(c + d, C)
+            send = remote(outgoing[j].at[to], landed[j].at[c], s5.at[j, d], r5.at[j, d], col=to)
+            send.start()
+            last[j].append(send)
+        landed[j][c] = outgoing[j][c]
+    for j, (at, size) in enumerate(cuts):
+        for send in last[j]:
+            send.wait_recv()
+        for p in range(C):
+            out_ref[:, p * ab + at:p * ab + at + size] = landed[j][p].astype(jnp.bfloat16)
+    for send in sends + pairs + sum(chips, []) + sum(last, []):
+        send.wait_send()
+
+
+def staged(R, C, N, amp_ref, sym_ij_ref, sym_ef_ref, panel_ref, out_ref,
            panel_v, slabs, met, rows16, gathered, allowed, part, from_pair, summed, from_chips, outgoing, landed,
            panel_sem, s1, r1, s2, r2, s3, r3, s4, r4, s5, r5):
     r = lax.axis_index("row")
@@ -96,48 +219,57 @@
             pick, everything, preferred_element_type=jnp.float32
         ).astype(jnp.bfloat16)
 
-    def multiply(half):
-        left = allowed[half]
-        for at, size in tiles(ab):
-            part[half, :, pl.ds(at, size)] = lax.dot_general(
-                left, panel_v[:, pl.ds(at, size)], (((1,), (0,)), ((), ())), preferred_element_type=jnp.float32
-            )
+    cuts = chunks(ab, N)
+
+    def multiply(half, j):
+        at, size = cuts[j]
+        part[j][half] = jnp.dot(allowed[half], panel_v[:, pl.ds(at, size)], preferred_element_type=jnp.float32)
 
     load.wait()
-    multiply(1 - k)
-    pair = remote(part.at[1 - k], from_pair, s3, r3, row=2 * q + 1 - k)
-    pair.start()
-    multiply(k)
-    pair.wait_recv()
-
-    for p in range(Q):
-        at = pl.ds(p * C * J, C * J)
-        summed[p] = part[k, at, :] + from_pair[at, :]
-    chips = []
-    for d in range(1, Q):
-        to = lax.rem(q + d, Q)
-        send = remote(summed.at[to], from_chips.at[d - 1], s4.at[d], r4.at[d], row=2 * to + k)
-        send.start()
-        chips.append(send)
-    total = summed[q]
-    for d, send in enumerate(chips):
-        send.wait_recv()
-        total = total + from_chips[d]
-    for p in range(C):
-        outgoing[p] = total[p * J:(p + 1) * J, :]
-    last = []
-    for d in range(1, C):
-        to = lax.rem(c + d, C)
-        send = remote(outgoing.at[to], landed.at[c], s5.at[d], r5.at[d], col=to)
-        send.start()
-        last.append(send)
-    landed[c] = outgoing[c]
-    for send in last:
-        send.wait_recv()
-    for p in range(C):
-        out_ref[:, p * ab:(p + 1) * ab] = landed[p].astype(jnp.bfloat16)
-    pair.wait_send()
-    for send in sends + more + chips + last:
+    pairs, chips, last = [], [], []
+
+    def reduce_pair(j):
+        pairs[j].wait_recv()
+        for p in range(Q):
+            at = pl.ds(p * C * J, C * J)
+            summed[j][p] = part[j][k, at, :] + from_pair[j][at, :]
+        chips.append([])
+        for d in range(1, Q):
+            to = lax.rem(q + d, Q)
+            send = remote(summed[j].at[to], from_chips[j].at[d - 1], s4.at[j, d], r4.at[j, d], row=2 * to + k)
+            send.start()
+            chips[j].append(send)
+
+    for j in range(len(cuts)):
+        multiply(1 - k, j)
+        pair = remote(part[j].at[1 - k], from_pair[j], s3.at[j], r3.at[j], row=2 * q + 1 - k)
+        pair.start()
+        pairs.append(pair)
+        multiply(k, j)
+        if j > 0:
+            reduce_pair(j - 1)
+    reduce_pair(len(cuts) - 1)
+
+    for j in range(len(cuts)):
+        total = summed[j][q]
+        for d, send in enumerate(chips[j]):
+            send.wait_recv()
+            total = total + from_chips[j][d]
+        for p in range(C):
+            outgoing[j][p] = total[p * J:(p + 1) * J, :]
+        last.append([])
+        for d in range(1, C):
+            to = lax.rem(c + d, C)
+            send = remote(outgoing[j].at[to], landed[j].at[c], s5.at[j, d], r5.at[j, d], col=to)
+            send.start()
+            last[j].append(send)
+        landed[j][c] = outgoing[j][c]
+    for j, (at, size) in enumerate(cuts):
+        for send in last[j]:
+            send.wait_recv()
+        for p in range(C):
+            out_ref[:, p * ab + at:p * ab + at + size] = landed[j][p].astype(jnp.bfloat16)
+    for send in sends + more + pairs + sum(chips, []) + sum(last, []):
         send.wait_send()
 
 
@@ -147,12 +279,32 @@
     def body(amplitudes, panel, irrep_ij, irrep_ef):
         J, EF = amplitudes.shape
         ab, ef = panel.shape
+        N = max(1, min(CHUNKS, ab // 512))
+        widths = [size for _, size in chunks(ab, N)]
         Q = R // 2
         H = Q * C * J
         f32, bf16 = jnp.float32, jnp.bfloat16
         dma = pltpu.SemaphoreType.DMA
+        if R * C <= 64 and J == 2 and ef <= 1024:
+            exchange = direct
+            buffers = [
+                pltpu.VMEM((R, J * 8, 128), f32),
+                pltpu.VMEM((R, J * 8, 128), bf16),
+                pltpu.VMEM((pl.cdiv(ef, 128), 2, H, R * C * J * 8), f32),
+                pltpu.VMEM((R * C, J * 8, 128), bf16),
+            ]
+            semaphores = [dma((R * C,)), dma((R * C,))]
+        else:
+            exchange = staged
+            buffers = [
+                pltpu.VMEM((R, J, ef), f32),
+                pltpu.VMEM((R, J, ef), f32),
+                pltpu.VMEM((R * J, ef), f32),
+                pltpu.VMEM((C, R * J, ef), bf16),
+            ]
+            semaphores = [dma((R,)), dma((R,)), dma((C,)), dma((C,))]
         return pl.pallas_call(
-            functools.partial(kernel, R, C),
+            functools.partial(exchange, R, C, N),
             out_shape=jax.ShapeDtypeStruct((J, C * ab), bf16),
             in_specs=[
                 pl.BlockSpec(memory_space=pltpu.VMEM),
@@ -163,23 +315,19 @@
             out_specs=pl.BlockSpec(memory_space=pltpu.VMEM),
             scratch_shapes=[
                 pltpu.VMEM((ef, ab), bf16),
-                pltpu.VMEM((R, J, ef), f32),
-                pltpu.VMEM((R, J, ef), f32),
-                pltpu.VMEM((R * J, ef), f32),
-                pltpu.VMEM((C, R * J, ef), bf16),
+                *buffers,
                 pltpu.VMEM((2, H, ef), bf16),
-                pltpu.VMEM((2, H, ab), f32),
-                pltpu.VMEM((H, ab), f32),
-                pltpu.VMEM((Q, C * J, ab), f32),
-                pltpu.VMEM((max(Q - 1, 1), C * J, ab), f32),
-                pltpu.VMEM((C, J, ab), f32),
-                pltpu.VMEM((C, J, ab), f32),
+                [pltpu.VMEM((2, H, w), f32) for w in widths],
+                [pltpu.VMEM((H, w), f32) for w in widths],
+                [pltpu.VMEM((Q, C * J, w), f32) for w in widths],
+                [pltpu.VMEM((max(Q - 1, 1), C * J, w), f32) for w in widths],
+                [pltpu.VMEM((C, J, w), f32) for w in widths],
+                [pltpu.VMEM((C, J, w), f32) for w in widths],
                 dma,
-                dma((R,)), dma((R,)),
-                dma((C,)), dma((C,)),
-                dma, dma,
-                dma((Q,)), dma((Q,)),
-                dma((C,)), dma((C,)),
+                *semaphores,
+                dma((N,)), dma((N,)),
+                dma((N, Q)), dma((N, Q)),
+                dma((N, C)), dma((N, C)),
             ],
             compiler_params=pltpu.CompilerParams(
                 collective_id=0, has_side_effects=True, vmem_limit_bytes=60 << 20

time: 28.6 us -> 27 us (0.944)
  Pallas kernels: 26.9 us -> 25.4 us
    pallas_call x1, Pallas kernels: 26.9 us -> 25.4 us  [body(): pl.pallas_call(functools.partial(exchange, R, C, N), out_shape=jax.ShapeD...]
where the time goes in v2:
time: 27 us; the launch traced here: 26.8 us
  Pallas kernels  25.4 us (94%)
  local copies, waits for them, and re-layouts  1.42 us (5%)
    pallas_call x1, Pallas kernels, body(): pl.pallas_call(functools.partial(exchange, R, C, N), out_shape=jax.ShapeD...  25.4 us
    unnamed x1, local copies, waits for them, and re-layouts  1.42 us

profile of v2, /device:TPU:0, one launch (start us, length us, event | category | flops | bytes accessed | tf_op | source)
XLA Modules:
  0.0 26.8 jit_solution(9911491134218021812)
XLA Ops:
  0.0 25.4 %shard_map.46 = bf16[2,9600]{1,0:T(2,128)(2,1)} custom-call(bf16[2,6400]{1,0:T(2,128)(2,1)} %amp_ref.1, s32[64]{0:T(128)} %sym_ij_ref.1, s32[6400]{0:T(1024)} %sym_ef_ref.1, bf16[800,2400]{1,0:T(8,128)(2,1)} %bitcast.1), custom_call_target="tpu_custom_call" | custom-call | flops 245760000 | bytes 3840000 | tf_op jit(solution)/shard_map/pallas_call | solution.py:306
  25.4 1.4 %copy.6 = bf16[2,9600]{1,0:T(2,128)(2,1)} copy(bf16[2,9600]{1,0:T(2,128)(2,1)} %shard_map.46) | data formatting | bytes 76800

commit v3 on v2

--- a/solution.py
+++ b/solution.py
@@ -23,8 +23,8 @@
 
 
 def direct(R, C, N, amp_ref, sym_ij_ref, sym_ef_ref, panel_ref, out_ref,
-           panel_v, wide, slabs, pick, gathered, allowed, part, from_pair, summed, from_chips, outgoing, landed,
-           panel_sem, s1, r1, s3, r3, s4, r4, s5, r5):
+           panel_v, wide, slabs, mate, both, pick, gathered, allowed, part, from_pair, summed, from_chips, outgoing, landed,
+           panel_sem, s1, r1, s2, r2, s3, r3, s4, r4, s5, r5):
     r = lax.axis_index("row")
     c = lax.axis_index("col")
     k = lax.rem(r, 2)
@@ -39,15 +39,25 @@
 
     lanes = [(at, min(128, ef - at)) for at in range(0, ef, 128)]
     L = 8
-    D = R * C
-    peers = [(dr, dc) for dc in reversed(range(C)) for dr in reversed(range(R)) if (dr, dc) != (0, 0)]
+    peers = [(dq, m) for m in range(C) for dq in range(Q) if (dq, m) != (0, 0)]
+
+    def partner(m):
+        col, bit = c, 1
+        while bit < C:
+            if m & bit:
+                col = col + bit - 2 * bit * lax.rem(c // bit, 2)
+            bit *= 2
+        return col
 
     barrier = pltpu.get_barrier_semaphore()
-    for dr, dc in peers:
+    for dq, m in peers:
         pl.semaphore_signal(
-            barrier, inc=1, device_id={"row": lax.rem(r + dr, R), "col": lax.rem(c + dc, C)},
+            barrier, inc=1, device_id={"row": 2 * lax.rem(q + dq, Q) + k, "col": partner(m)},
             device_id_type=pl.DeviceIdType.MESH,
         )
+    pl.semaphore_signal(
+        barrier, inc=1, device_id={"row": 2 * q + 1 - k}, device_id_type=pl.DeviceIdType.MESH
+    )
 
     first = (c * R + r) * J
     sym_ef = sym_ef_ref[...].reshape(1, EF)
@@ -61,86 +71,90 @@
         for i, (at, size) in enumerate(lanes):
             for j in range(J):
                 wide[p, j * L + i:j * L + i + 1, 0:size] = masked[j:j + 1, p * ef + at:p * ef + at + size]
-    slabs[...] = wide[...].astype(jnp.bfloat16)
-
-    at = lax.broadcasted_iota(jnp.int32, (C * J, D * J * L), 0)
-    held = lax.broadcasted_iota(jnp.int32, (C * J, D * J * L), 1)
-    base = (at // J) * (R * J * L) + lax.rem(at, J) * L
+    for p in range(R):
+        slabs[p % 2, p // 2] = wide[p].astype(jnp.bfloat16)
+
+    pl.semaphore_wait(barrier, Q * C)
+
+    swap = remote(slabs.at[1 - k], mate, s2, r2, row=2 * q + 1 - k)
+    swap.start()
+    for p in range(Q):
+        both[p, k] = slabs[k, p]
+    swap.wait_recv()
+    for p in range(Q):
+        both[p, 1 - k] = mate[p]
+
+    sends = []
+    for dq, m in peers:
+        to = lax.rem(q + dq, Q)
+        send = remote(both.at[to], gathered.at[c, q], s1.at[m, dq], r1.at[m, dq], row=2 * to + k, col=partner(m))
+        send.start()
+        sends.append((m, send))
+    gathered[c, q] = both[q]
+    held = lax.broadcasted_iota(jnp.int32, (J, R * J * L), 1)
+    base = lax.broadcasted_iota(jnp.int32, (J, R * J * L), 0) * L
     for half in range(2):
         for p in range(Q):
             for i in range(len(lanes)):
-                pick[i, half, pl.ds(p * C * J, C * J), :] = jnp.where(
+                pick[i, pl.ds((half * Q + p) * J, J), :] = jnp.where(
                     base + ((2 * p + half) * J * L + i) == held, 1.0, 0.0)
-    picks = pick[...].reshape(len(lanes) * D * J, D * J * L).astype(jnp.bfloat16)
-
-    pl.semaphore_wait(barrier, D - 1)
-
-    sends = []
-    for dr, dc in peers:
-        row, col = lax.rem(r + dr, R), lax.rem(c + dc, C)
-        send = remote(slabs.at[row], gathered.at[c * R + r], s1.at[dc * R + dr], r1.at[dc * R + dr], row=row, col=col)
-        send.start()
-        sends.append(send)
-    gathered[c * R + r] = slabs[r]
-    for send in sends:
-        send.wait_recv()
-    picked = jnp.dot(picks, gathered[...].reshape(D * J * L, 128), preferred_element_type=jnp.float32)
-    for i, (at, size) in enumerate(lanes):
-        for half in range(2):
-            start = (i * 2 + half) * Q * C * J
-            allowed[half, :, at:at + size] = picked[start:start + Q * C * J, :size].astype(jnp.bfloat16)
-
-    cuts = chunks(ab, N)
-
-    def multiply(half, j):
-        at, size = cuts[j]
-        part[j][half] = jnp.dot(allowed[half], panel_v[:, pl.ds(at, size)], preferred_element_type=jnp.float32)
-
-    load.wait()
+    picks = pick[...].reshape(len(lanes) * R * J, R * J * L).astype(jnp.bfloat16)
+
     pairs, chips, last = [], [], []
 
-    def reduce_pair(j):
-        pairs[j].wait_recv()
+    def finish_pair(m):
+        pairs[m].wait_recv()
+        both_cores = part[m, k] + from_pair[m]
+        chips.append([])
         for p in range(Q):
-            at = pl.ds(p * C * J, C * J)
-            summed[j][p] = part[j][k, at, :] + from_pair[j][at, :]
-        chips.append([])
+            summed[m, p] = both_cores[p * J:(p + 1) * J, :]
         for d in range(1, Q):
             to = lax.rem(q + d, Q)
-            send = remote(summed[j].at[to], from_chips[j].at[d - 1], s4.at[j, d], r4.at[j, d], row=2 * to + k)
+            send = remote(summed.at[m, to], from_chips.at[m, d - 1], s4.at[m, d], r4.at[m, d], row=2 * to + k)
             send.start()
-            chips[j].append(send)
-
-    for j in range(len(cuts)):
-        multiply(1 - k, j)
-        pair = remote(part[j].at[1 - k], from_pair[j], s3.at[j], r3.at[j], row=2 * q + 1 - k)
+            chips[m].append(send)
+
+    def finish_chips(m):
+        total = summed[m, q]
+        for d, send in enumerate(chips[m]):
+            send.wait_recv()
+            total = total + from_chips[m, d]
+        if m == 0:
+            landed[c] = total
+            return
+        outgoing[m] = total
+        send = remote(outgoing.at[m], landed.at[c], s5.at[m], r5.at[m], col=partner(m))
+        send.start()
+        last.append(send)
+
+    for m in range(C):
+        for n, send in sends:
+            if n == m:
+                send.wait_recv()
+        block = gathered[partner(m)].reshape(R * J * L, 128)
+        picked = jnp.dot(picks, block, preferred_element_type=jnp.float32)
+        for i, (at, size) in enumerate(lanes):
+            allowed[m, :, at:at + size] = picked[i * R * J:(i + 1) * R * J, :size].astype(jnp.bfloat16)
+        if m == 0:
+            load.wait()
+        left = allowed[m]
+        for at, size in chunks(ab, N):
+            product = jnp.dot(left, panel_v[:, pl.ds(at, size)], preferred_element_type=jnp.float32)
+            part[m, 0, :, pl.ds(at, size)] = product[:Q * J]
+            part[m, 1, :, pl.ds(at, size)] = product[Q * J:]
+        pair = remote(part.at[m, 1 - k], from_pair.at[m], s3.at[m], r3.at[m], row=2 * q + 1 - k)
         pair.start()
         pairs.append(pair)
-        multiply(k, j)
-        if j > 0:
-            reduce_pair(j - 1)
-    reduce_pair(len(cuts) - 1)
-
-    for j in range(len(cuts)):
-        total = summed[j][q]
-        for d, send in enumerate(chips[j]):
-            send.wait_recv()
-            total = total + from_chips[j][d]
-        for p in range(C):
-            outgoing[j][p] = total[p * J:(p + 1) * J, :]
-        last.append([])
-        for d in range(1, C):
-            to = lax.rem(c + d, C)
-            send = remote(outgoing[j].at[to], landed[j].at[c], s5.at[j, d], r5.at[j, d], col=to)
-            send.start()
-            last[j].append(send)
-        landed[j][c] = outgoing[j][c]
-    for j, (at, size) in enumerate(cuts):
-        for send in last[j]:
-            send.wait_recv()
-        for p in range(C):
-            out_ref[:, p * ab + at:p * ab + at + size] = landed[j][p].astype(jnp.bfloat16)
-    for send in sends + pairs + sum(chips, []) + sum(last, []):
+        if m > 0:
+            finish_pair(m - 1)
+    finish_pair(C - 1)
+    for m in range(C):
+        finish_chips(m)
+    for send in last:
+        send.wait_recv()
+    for p in range(C):
+        out_ref[:, p * ab:(p + 1) * ab] = landed[p].astype(jnp.bfloat16)
+    for send in [send for _, send in sends] + [swap] + pairs + sum(chips, []) + last:
         send.wait_send()
 
 
@@ -285,15 +299,24 @@
         H = Q * C * J
         f32, bf16 = jnp.float32, jnp.bfloat16
         dma = pltpu.SemaphoreType.DMA
-        if R * C <= 64 and J == 2 and ef <= 1024:
+        if C & (C - 1) == 0 and 2 <= Q <= 4 and J == 2 and ef <= 1024:
             exchange = direct
             buffers = [
                 pltpu.VMEM((R, J * 8, 128), f32),
-                pltpu.VMEM((R, J * 8, 128), bf16),
-                pltpu.VMEM((pl.cdiv(ef, 128), 2, H, R * C * J * 8), f32),
-                pltpu.VMEM((R * C, J * 8, 128), bf16),
+                pltpu.VMEM((2, Q, J * 8, 128), bf16),
+                pltpu.VMEM((Q, J * 8, 128), bf16),
+                pltpu.VMEM((Q, 2, J * 8, 128), bf16),
+                pltpu.VMEM((pl.cdiv(ef, 128), R * J, R * J * 8), f32),
+                pltpu.VMEM((C, Q, 2, J * 8, 128), bf16),
+                pltpu.VMEM((C, R * J, ef), bf16),
+                pltpu.VMEM((C, 2, Q * J, ab), f32),
+                pltpu.VMEM((C, Q * J, ab), f32),
+                pltpu.VMEM((C, Q, J, ab), f32),
+                pltpu.VMEM((C, Q - 1, J, ab), f32),
+                pltpu.VMEM((C, J, ab), f32),
+                pltpu.VMEM((C, J, ab), f32),
             ]
-            semaphores = [dma((R * C,)), dma((R * C,))]
+            semaphores = [dma((C, Q)), dma((C, Q)), dma, dma, dma((C,)), dma((C,)), dma((C, Q)), dma((C, Q)), dma((C,)), dma((C,))]
         else:
             exchange = staged
             buffers = [
@@ -301,8 +324,20 @@
                 pltpu.VMEM((R, J, ef), f32),
                 pltpu.VMEM((R * J, ef), f32),
                 pltpu.VMEM((C, R * J, ef), bf16),
+                pltpu.VMEM((2, H, ef), bf16),
+                [pltpu.VMEM((2, H, w), f32) for w in widths],
+                [pltpu.VMEM((H, w), f32) for w in widths],
+                [pltpu.VMEM((Q, C * J, w), f32) for w in widths],
+                [pltpu.VMEM((max(Q - 1, 1), C * J, w), f32) for w in widths],
+                [pltpu.VMEM((C, J, w), f32) for w in widths],
+                [pltpu.VMEM((C, J, w), f32) for w in widths],
             ]
-            semaphores = [dma((R,)), dma((R,)), dma((C,)), dma((C,))]
+            semaphores = [
+                dma((R,)), dma((R,)), dma((C,)), dma((C,)),
+                dma((N,)), dma((N,)),
+                dma((N, Q)), dma((N, Q)),
+                dma((N, C)), dma((N, C)),
+            ]
         return pl.pallas_call(
             functools.partial(exchange, R, C, N),
             out_shape=jax.ShapeDtypeStruct((J, C * ab), bf16),
@@ -316,18 +351,8 @@
             scratch_shapes=[
                 pltpu.VMEM((ef, ab), bf16),
                 *buffers,
-                pltpu.VMEM((2, H, ef), bf16),
-                [pltpu.VMEM((2, H, w), f32) for w in widths],
-                [pltpu.VMEM((H, w), f32) for w in widths],
-                [pltpu.VMEM((Q, C * J, w), f32) for w in widths],
-                [pltpu.VMEM((max(Q - 1, 1), C * J, w), f32) for w in widths],
-                [pltpu.VMEM((C, J, w), f32) for w in widths],
-                [pltpu.VMEM((C, J, w), f32) for w in widths],
                 dma,
                 *semaphores,
-                dma((N,)), dma((N,)),
-                dma((N, Q)), dma((N, Q)),
-                dma((N, C)), dma((N, C)),
             ],
             compiler_params=pltpu.CompilerParams(
                 collective_id=0, has_side_effects=True, vmem_limit_bytes=60 << 20

time: 27 us -> 26.2 us (0.970)
  Pallas kernels: 25.4 us -> 24.5 us
    pallas_call x1, Pallas kernels: 25.4 us -> 24.5 us  [body(): pl.pallas_call(functools.partial(exchange, R, C, N), out_shape=jax.ShapeD...]
where the time goes in v3:
time: 26.2 us; the launch traced here: 25.9 us
  Pallas kernels  24.5 us (94%)
  local copies, waits for them, and re-layouts  1.42 us (5%)
    pallas_call x1, Pallas kernels, body(): pl.pallas_call(functools.partial(exchange, R, C, N), out_shape=jax.ShapeD...  24.5 us
    unnamed x1, local copies, waits for them, and re-layouts  1.42 us

profile of v3, /device:TPU:0, one launch (start us, length us, event | category | flops | bytes accessed | tf_op | source)
XLA Modules:
  0.0 25.9 jit_solution(8707241032463072118)
XLA Ops:
  0.0 24.5 %shard_map.46 = bf16[2,9600]{1,0:T(2,128)(2,1)} custom-call(bf16[2,6400]{1,0:T(2,128)(2,1)} %amp_ref.1, s32[64]{0:T(128)} %sym_ij_ref.1, s32[6400]{0:T(1024)} %sym_ef_ref.1, bf16[800,2400]{1,0:T(8,128)(2,1)} %bitcast.1), custom_call_target="tpu_custom_call" | custom-call | flops 245760000 | bytes 3840000 | tf_op jit(solution)/shard_map/pallas_call | solution.py:341
  24.5 1.4 %copy.6 = bf16[2,9600]{1,0:T(2,128)(2,1)} copy(bf16[2,9600]{1,0:T(2,128)(2,1)} %shard_map.46) | data formatting | bytes 76800
